TPU v7x, 32 devices: a whole 2x2x4 slice. The times are simulated.
32 devices in a mesh: replica: 8 (over y, x, core), shard: 4 (over z).
Axes of the slice: x: 2, y: 2, z: 4, core: 2. Of those that a mesh axis runs over, the one named last changes fastest.
Arguments:
- tokens: bfloat16 [4096, 960], P(('replica', 'shard')), may hold values from -6 to 6
- seq_lengths: int32 [32, 3], P(('replica', 'shard')), may hold values from 1 to 64, 128 in all within a row
- norm_one: bfloat16 [960], P('shard'), may hold values from 0.099609375 to 1.8984375
- query_weight: bfloat16 [960, 960], P('shard'), may hold values from -0.1875 to 0.1875
- key_weight: bfloat16 [960, 320], P('shard'), may hold values from -0.1875 to 0.1875
- value_weight: bfloat16 [960, 320], P('shard'), may hold values from -0.1875 to 0.1875
- output_weight: bfloat16 [960, 960], P('shard'), may hold values from -0.75 to 0.75
- norm_two: bfloat16 [960], P('shard'), may hold values from 0.099609375 to 1.8984375
- gate_weight: bfloat16 [960, 2560], P('shard'), may hold values from -0.1875 to 0.1875
- up_weight: bfloat16 [960, 2560], P('shard'), may hold values from -0.1875 to 0.1875
- down_weight: bfloat16 [2560, 960], P('shard'), may hold values from -0.125 to 0.125
- out_grad: bfloat16 [4096, 960], P(('replica', 'shard')), may hold values from -6 to 6
Outputs:
- mixed: bfloat16 [4096, 960], P(('replica', 'shard'))
- input_grad: float32 [4096, 960], P(('replica', 'shard'))
- norm_one_grad: float32 [960], P('shard')
- query_grad: float32 [960, 960], P('shard')
- key_grad: float32 [960, 320], P('shard')
- value_grad: float32 [960, 320], P('shard')
- output_grad: float32 [960, 960], P('shard')
- norm_two_grad: float32 [960], P('shard')
- gate_grad: float32 [960, 2560], P('shard')
- up_grad: float32 [960, 2560], P('shard')
- down_grad: float32 [2560, 960], P('shard')
Inputs may be any that keep to these rules, and one draw needn't show every extreme that they name: `seq_lengths`: each device's row sums to 128, and its longest sequence has exactly 64 tokens.
All inputs are finite; a program needn't handle non-finite values.
Results may differ from a plain program's by a relative error of at most 0.013.
Values may be sent and summed in bfloat16 or wider, within the bound.
A program may use at most 128 MiB of HBM per device.

v0:
```python
import math

import jax
import jax.numpy as jnp
from jax import lax
from jax.sharding import PartitionSpec as P

HEADS = 15
KV_HEADS = 5
HEAD = 64


EPSILON = 1e-05
THETA = 100000.0


def layout(length_row, count):
    index_row = jnp.arange(count, dtype=jnp.int32)
    seq_ends = jnp.cumsum(length_row)
    seq_starts = seq_ends - length_row
    doc_index = jnp.sum((index_row[:, None] >= seq_ends[None, :]).astype(jnp.int32), axis=1)
    one_hot = doc_index[:, None] == jnp.arange(length_row.shape[0], dtype=jnp.int32)[None, :]
    first_slot = jnp.sum(jnp.where(one_hot, seq_starts[None, :], 0), axis=1)
    return (doc_index, index_row - first_slot)


def tables(positions, head_size):
    half_size = head_size // 2
    freq_index = jnp.arange(half_size, dtype=jnp.float32)
    inverse = THETA ** (-2.0 * freq_index / head_size)
    angles = positions.astype(jnp.float32)[..., None] * inverse
    return (jnp.cos(angles), jnp.sin(angles))


def rotate(values, cosine, sine):
    half_size = values.shape[-1] // 2
    first_half = values[..., :half_size]
    second_half = values[..., half_size:]
    cos_heads = cosine[:, None, :]
    sin_heads = sine[:, None, :]
    return jnp.concatenate(
        [
            first_half * cos_heads - second_half * sin_heads,
            second_half * cos_heads + first_half * sin_heads,
        ],
        axis=-1,
    )


def unrotate(grads, cosine, sine):
    half_size = grads.shape[-1] // 2
    first_half = grads[..., :half_size]
    second_half = grads[..., half_size:]
    cos_heads = cosine[:, None, :]
    sin_heads = sine[:, None, :]
    return jnp.concatenate(
        [
            first_half * cos_heads + second_half * sin_heads,
            second_half * cos_heads - first_half * sin_heads,
        ],
        axis=-1,
    )


def matmul(left, right):
    return jnp.dot(left, right, preferred_element_type=jnp.float32)


def matmul_right_t(left, right):
    return jnp.einsum("te,de->td", left, right, preferred_element_type=jnp.float32)


def matmul_left_t(left, right):
    return jnp.einsum("td,te->de", left, right, preferred_element_type=jnp.float32)


def masked_scores(query_rot, key_rot, allowed, score_scale):
    raw_scores = jnp.einsum(
        "tkhd,skd->khts", query_rot, key_rot, preferred_element_type=jnp.float32
    )
    return jnp.where(allowed[None, None], raw_scores * score_scale, -1e30)


def on_device(
    tokens,
    seq_lengths,
    norm_one,
    query_weight,
    key_weight,
    value_weight,
    output_weight,
    norm_two,
    gate_weight,
    up_weight,
    down_weight,
    out_grad,
):
    count, width = tokens.shape
    group_heads = HEADS // KV_HEADS
    score_scale = 1.0 / math.sqrt(HEAD)
    doc_index, positions = layout(seq_lengths[0], count)
    cosine, sine = tables(positions, HEAD)
    slots = jnp.arange(count, dtype=jnp.int32)
    allowed = (doc_index[:, None] == doc_index[None, :]) & (slots[:, None] >= slots[None, :])
    gain_one, wide_query, wide_key, wide_value, wide_output = (
        lax.all_gather(norm_one, "shard", axis=0, tiled=True),
        lax.all_gather(query_weight, "shard", axis=0, tiled=True),
        lax.all_gather(key_weight, "shard", axis=0, tiled=True),
        lax.all_gather(value_weight, "shard", axis=0, tiled=True),
        lax.all_gather(output_weight, "shard", axis=0, tiled=True),
    )
    hidden_in = tokens.astype(jnp.float32)
    scale_one = lax.rsqrt(jnp.mean(hidden_in * hidden_in, axis=-1, keepdims=True) + EPSILON)
    normed_one = (hidden_in * scale_one * gain_one.astype(jnp.float32)).astype(jnp.bfloat16)
    queries_pre = matmul(normed_one, wide_query).reshape(count, HEADS, HEAD)
    query_rot = (
        rotate(queries_pre, cosine, sine)
        .astype(jnp.bfloat16)
        .reshape(count, KV_HEADS, group_heads, HEAD)
    )
    keys_pre = matmul(normed_one, wide_key).reshape(count, KV_HEADS, HEAD)
    key_rot = rotate(keys_pre, cosine, sine).astype(jnp.bfloat16)
    value_rot = matmul(normed_one, wide_value).astype(jnp.bfloat16).reshape(count, KV_HEADS, HEAD)
    scores = masked_scores(query_rot, key_rot, allowed, score_scale)
    log_total = jax.nn.logsumexp(scores, axis=-1, keepdims=True)
    probs_low = jnp.exp(scores - log_total).astype(jnp.bfloat16)
    context = jnp.einsum("khts,skd->tkhd", probs_low, value_rot, preferred_element_type=jnp.float32)
    context = context.reshape(count, width).astype(jnp.bfloat16)
    after_attn = hidden_in + matmul(context, wide_output)
    gain_two, wide_gate, wide_up, wide_down = (
        lax.all_gather(norm_two, "shard", axis=0, tiled=True),
        lax.all_gather(gate_weight, "shard", axis=0, tiled=True),
        lax.all_gather(up_weight, "shard", axis=0, tiled=True),
        lax.all_gather(down_weight, "shard", axis=0, tiled=True),
    )
    scale_two = lax.rsqrt(jnp.mean(after_attn * after_attn, axis=-1, keepdims=True) + EPSILON)
    normed_two = (after_attn * scale_two * gain_two.astype(jnp.float32)).astype(jnp.bfloat16)
    gate_pre = matmul(normed_two, wide_gate)
    up_pre = matmul(normed_two, wide_up)
    sigmoid_gate = jax.nn.sigmoid(gate_pre)
    silu_gate = gate_pre * sigmoid_gate
    act = (silu_gate * up_pre).astype(jnp.bfloat16)
    mixed = (after_attn + matmul(act, wide_down)).astype(jnp.bfloat16)
    cotangent = out_grad.astype(jnp.float32)
    act_grad = matmul_right_t(out_grad, wide_down)
    gate_back = (act_grad * up_pre * sigmoid_gate * (1.0 + gate_pre * (1.0 - sigmoid_gate))).astype(
        jnp.bfloat16
    )
    up_back = (act_grad * silu_gate).astype(jnp.bfloat16)
    normed_two_grad = matmul_right_t(gate_back, wide_gate) + matmul_right_t(up_back, wide_up)
    gain_two_sum = jnp.sum(normed_two_grad * after_attn * scale_two, axis=0)
    weighted_two = normed_two_grad * gain_two.astype(jnp.float32)
    attn_out_grad = (
        cotangent
        + scale_two * weighted_two
        - after_attn * scale_two**3 * jnp.mean(after_attn * weighted_two, axis=-1, keepdims=True)
    )
    normed_cols, act_cols = (
        lax.all_to_all(normed_two, "shard", split_axis=1, concat_axis=0, tiled=True),
        lax.all_to_all(act, "shard", split_axis=1, concat_axis=0, tiled=True),
    )
    gate_piece = lax.all_gather(gate_back, "shard", axis=0, tiled=True)
    up_piece = lax.all_gather(up_back, "shard", axis=0, tiled=True)
    cot_piece = lax.all_gather(out_grad, "shard", axis=0, tiled=True)
    gate_own = matmul_left_t(normed_cols, gate_piece)
    up_own = matmul_left_t(normed_cols, up_piece)
    down_own = matmul_left_t(act_cols, cot_piece)
    gain_two_own = lax.psum_scatter(gain_two_sum, "shard", scatter_dimension=0, tiled=True)
    feed_shards = (gain_two_own, gate_own, up_own, down_own)
    attn_low = attn_out_grad.astype(jnp.bfloat16)
    output_sum = matmul_left_t(context, attn_low)
    context_grad = (
        matmul_right_t(attn_low, wide_output)
        .astype(jnp.bfloat16)
        .reshape(count, KV_HEADS, group_heads, HEAD)
    )
    scores = masked_scores(query_rot, key_rot, allowed, score_scale)
    probs = jnp.exp(scores - log_total)
    probs_low = probs.astype(jnp.bfloat16)
    value_back = jnp.einsum(
        "khts,tkhd->skd", probs_low, context_grad, preferred_element_type=jnp.float32
    )
    value_back = value_back.reshape(count, KV_HEADS * HEAD).astype(jnp.bfloat16)
    probs_grad = jnp.einsum(
        "tkhd,skd->khts", context_grad, value_rot, preferred_element_type=jnp.float32
    )
    row_inner = jnp.sum(probs * probs_grad, axis=-1, keepdims=True)
    score_back = (probs * (probs_grad - row_inner) * score_scale).astype(jnp.bfloat16)
    query_rot_grad = jnp.einsum(
        "khts,skd->tkhd", score_back, key_rot, preferred_element_type=jnp.float32
    )
    key_rot_grad = jnp.einsum(
        "khts,tkhd->skd", score_back, query_rot, preferred_element_type=jnp.float32
    )
    query_back = (
        unrotate(query_rot_grad.reshape(count, HEADS, HEAD), cosine, sine)
        .reshape(count, width)
        .astype(jnp.bfloat16)
    )
    key_back = (
        unrotate(key_rot_grad, cosine, sine).reshape(count, KV_HEADS * HEAD).astype(jnp.bfloat16)
    )
    query_sum = matmul_left_t(normed_one, query_back)
    key_sum = matmul_left_t(normed_one, key_back)
    value_sum = matmul_left_t(normed_one, value_back)
    normed_one_grad = (
        matmul_right_t(query_back, wide_query)
        + matmul_right_t(key_back, wide_key)
        + matmul_right_t(value_back, wide_value)
    )
    gain_one_sum = jnp.sum(normed_one_grad * hidden_in * scale_one, axis=0)
    weighted_one = normed_one_grad * gain_one.astype(jnp.float32)
    input_grad = (
        attn_out_grad
        + scale_one * weighted_one
        - hidden_in * scale_one**3 * jnp.mean(hidden_in * weighted_one, axis=-1, keepdims=True)
    )
    attn_shards = (
        lax.psum_scatter(gain_one_sum, "shard", scatter_dimension=0, tiled=True),
        lax.psum_scatter(query_sum, "shard", scatter_dimension=0, tiled=True),
        lax.psum_scatter(key_sum, "shard", scatter_dimension=0, tiled=True),
        lax.psum_scatter(value_sum, "shard", scatter_dimension=0, tiled=True),
        lax.psum_scatter(output_sum, "shard", scatter_dimension=0, tiled=True),
    )
    members = (
        attn_shards[0],
        attn_shards[1],
        attn_shards[2],
        attn_shards[3],
        attn_shards[4],
        feed_shards[0],
        feed_shards[1],
        feed_shards[2],
        feed_shards[3],
    )
    flat_grads = jnp.concatenate([member.reshape(-1) for member in members])
    used_len = flat_grads.shape[0]
    tile_span = lax.axis_size("replica") * 128
    padded_len = -(-used_len // tile_span) * tile_span
    flat_grads = jnp.pad(flat_grads, (0, padded_len - used_len))
    own_part = lax.psum_scatter(flat_grads, "replica", scatter_dimension=0, tiled=True)
    whole_sum = lax.all_gather(own_part, "replica", axis=0, tiled=True)
    unpacked = []
    offset = 0
    for member in members:
        unpacked.append(whole_sum[offset : offset + member.size].reshape(member.shape))
        offset = offset + member.size
    return (
        mixed,
        input_grad,
        unpacked[0],
        unpacked[1],
        unpacked[2],
        unpacked[3],
        unpacked[4],
        unpacked[5],
        unpacked[6],
        unpacked[7],
        unpacked[8],
    )


def solution(mesh):
    in_specs = (
        P(("replica", "shard"), None),
        P(("replica", "shard"), None),
        P("shard"),
        P("shard", None),
        P("shard", None),
        P("shard", None),
        P("shard", None),
        P("shard"),
        P("shard", None),
        P("shard", None),
        P("shard", None),
        P(("replica", "shard"), None),
    )
    out_specs = (
        P(("replica", "shard"), None),
        P(("replica", "shard"), None),
        P("shard"),
        P("shard", None),
        P("shard", None),
        P("shard", None),
        P("shard", None),
        P("shard"),
        P("shard", None),
        P("shard", None),
        P("shard", None),
    )
    return jax.shard_map(
        on_device, mesh=mesh, in_specs=in_specs, out_specs=out_specs, check_vma=False
    )
```

profile of v0, /device:TPU:0, one launch (start us, length us, event | category | flops | bytes accessed | tf_op | source)
XLA Modules:
  0.0 1113.3 jit_solution(10009931821174036080)
XLA Ops:
  10.7 24.4 %all-gather = bf16[4,240,320]{1,2,0:T(8,128)(2,1)S(1)} all-gather(bf16[1,240,320]{1,2,0:T(8,128)(2,1)S(1)} %bitcast.143), channel_id=1, replica_groups=mesh['replica'=8,'shard'=4] {'shard'}, dimensions={0}, use_global_device_ids=true | all-gather | bytes 768000 | tf_op jit(solution)/shard_map/all_gather | solution.py:109
  38.0 12.1 %all-reduce.7 = (bf16[960]{0:T(1024)(128)(2,1)S(1)}, bf16[960]{0:T(1024)(128)(2,1)S(1)}) all-reduce(bf16[960]{0:T(1024)(128)(2,1)S(1)} %dynamic-update-slice, bf16[960]{0:T(1024)(128)(2,1)S(1)} %dynamic-update-slice.1), channel_id=1, replica_groups=mesh['replica'=8,'shard'=4] {'shard'}, use_global_device_ids=true, to_apply=%add.1 | all-reduce | flops 1920 | bytes 7680
  50.1 21.7 %all-gather.1 = bf16[4,240,320]{1,2,0:T(8,128)(2,1)S(1)} all-gather(bf16[1,240,320]{1,2,0:T(8,128)(2,1)S(1)} %bitcast.144), channel_id=1, replica_groups=mesh['replica'=8,'shard'=4] {'shard'}, dimensions={0}, use_global_device_ids=true | all-gather | bytes 768000 | tf_op jit(solution)/shard_map/all_gather | solution.py:108
  79.0 36.0 %all-gather.14.cloned.1.call-done = bf16[960,960]{1,0:T(8,128)(2,1)} async-done(((bf16[240,960]{1,0:T(8,128)(2,1)}), bf16[960,960]{1,0:T(8,128)(2,1)}) %all-gather.14.cloned.1.call-update) | async-done | bytes 1843216 | tf_op jit(solution)/shard_map/all_gather | solution.py:110
  118.9 89.2 %all-gather.16.cloned.1.call-done = bf16[960,2560]{1,0:T(8,128)(2,1)} async-done(((bf16[240,2560]{1,0:T(8,128)(2,1)}), bf16[960,2560]{1,0:T(8,128)(2,1)}) %all-gather.16.cloned.1.call-update) | async-done | bytes 4915216 | tf_op jit(solution)/shard_map/all_gather | solution.py:132
  212.5 88.1 %all-gather.18.cloned.1.call-done = bf16[960,2560]{1,0:T(8,128)(2,1)} async-done(((bf16[240,2560]{1,0:T(8,128)(2,1)}), bf16[960,2560]{1,0:T(8,128)(2,1)}) %all-gather.18.cloned.1.call-update) | async-done | bytes 4915216 | tf_op jit(solution)/shard_map/all_gather | solution.py:133
  305.1 88.1 %all-gather.20.cloned.1.call-done = bf16[2560,960]{0,1:T(8,128)(2,1)} async-done(((bf16[640,960]{0,1:T(8,128)(2,1)}), bf16[2560,960]{0,1:T(8,128)(2,1)}) %all-gather.20.cloned.1.call-update) | async-done | bytes 4915216 | tf_op jit(solution)/shard_map/all_gather | solution.py:134
  393.1 5.4 multiply_convert_fusion
  398.5 4.5 fusion.71
  403.1 4.7 multiply_reduce_fusion.1
  433.8 60.4 %all_gather.50 = bf16[512,960]{0,1:T(8,128)(2,1)} all-gather(bf16[128,960]{0,1:T(8,128)(2,1)} %param.23), channel_id=1, replica_groups=mesh['replica'=8,'shard'=4] {'shard'}, dimensions={0}, use_global_device_ids=true | all-gather | bytes 1228800 | tf_op jit(solution)/shard_map/all_gather | solution.py:164
  497.6 16.7 %all-to-all-start = ((bf16[128,4,240]{0,2,1:T(8,128)(2,1)}), bf16[128,4,240]{0,2,1:T(8,128)(2,1)}, u32[]{:S(2)}, u32[]{:S(2)}) async-start(bf16[128,4,240]{0,2,1:T(8,128)(2,1)} %bitcast.39), calls=%async_computation.2 | async-start | bytes 491520 | tf_op jit(solution)/shard_map/all_to_all | solution.py:159
  517.0 12.9 %all-reduce.6 = (f32[960]{0:T(1024)S(1)}, f32[960]{0:T(1024)S(1)}) all-reduce(f32[960]{0:T(1024)S(1)} %get-tuple-element.46, f32[960]{0:T(1024)S(1)} %copy-done.42), channel_id=2, replica_groups=mesh['replica'=8,'shard'=4] {'shard'}, use_global_device_ids=true, to_apply=%region_11.12.clone | all-reduce | flops 1920 | bytes 15360
  538.1 28.6 %all-gather.22.cloned.1.call-done = bf16[512,2560]{1,0:T(8,128)(2,1)} async-done(((bf16[128,2560]{1,0:T(8,128)(2,1)}), bf16[512,2560]{1,0:T(8,128)(2,1)}) %all-gather.22.cloned.1.call-update) | async-done | bytes 2621456 | tf_op jit(solution)/shard_map/all_gather | solution.py:162
  570.9 50.8 %all-gather.24.cloned.1.call-done = bf16[512,2560]{1,0:T(8,128)(2,1)} async-done(((bf16[128,2560]{1,0:T(8,128)(2,1)}), bf16[512,2560]{1,0:T(8,128)(2,1)}) %all-gather.24.cloned.1.call-update) | async-done | bytes 2621456 | tf_op jit(solution)/shard_map/all_gather | solution.py:163
  626.0 69.3 %reduce-scatter.9.cloned.1.call-done = f32[240,960]{1,0:T(8,128)} async-done(((f32[960,960]{1,0:T(8,128)}), f32[240,960]{1,0:T(8,128)}) %reduce-scatter.9.cloned.1.call-update) | async-done | bytes 921616 | tf_op jit(solution)/shard_map/reduce_scatter | solution.py:220
  698.0 72.8 %reduce-scatter.11.cloned.1.call-done = f32[240,960]{1,0:T(8,128)} async-done(((f32[960,960]{1,0:T(8,128)}), f32[240,960]{1,0:T(8,128)}) %reduce-scatter.11.cloned.1.call-update) | async-done | bytes 921616 | tf_op jit(solution)/shard_map/reduce_scatter | solution.py:223
  773.4 81.9 %concatenate.30 = f32[2458080]{0:T(1024)} concatenate(f32[240]{0:T(256)S(1)} %dynamic-slice.3, f32[230400]{0:T(1024)} %reshape.269, f32[76800]{0:T(1024)S(1)} %reshape.270, f32[76800]{0:T(1024)} %reshape.271, f32[230400]{0:T(1024)} %reshape.272, f32[240]{0:T(256)S(1)} %dynamic-slice.5, f32[614400]{0:T(1024)} %reshape.273, f32[614400]{0:T(1024)} %reshape.274, f32[614400]{0:T(1024)S(1)} %copy-done.1), dimensions={0} | concatenate | bytes 19664640 | tf_op jit(solution)/shard_map/concatenate | solution.py:236
  855.3 8.9 pad.4
  866.1 141.8 %all-reduce.10.cloned.1.call-done = f32[2458624]{0:T(1024)} async-done(((f32[2458624]{0:T(1024)}), f32[2458624]{0:T(1024)}) %all-reduce.10.cloned.1.call-update) | async-done | bytes 9834512
  1009.6 6.5 reshape.293
  1017.1 4.5 fusion.9
  1021.7 55.1 %all-gather.26.cloned.1.call-done = f32[8,1,307328]{2,1,0:T(1,128)} async-done(((f32[1,1,307328]{2,1,0:T(1,128)}), f32[8,1,307328]{2,1,0:T(1,128)}) %all-gather.26.cloned.1.call-update) | async-done | bytes 9834512 | tf_op jit(solution)/shard_map/all_gather | solution.py:242
  1082.6 7.4 fusion.63
  (220 shorter events, 105.0 us)
Async XLA Ops:
  7.2 68.0 %all-gather.12.cloned.1.call-start = ((), (), s32[]{:S(2)}) async-start(), calls=%async_computation.6 | async-start | bytes 2457600 | tf_op jit(solution)/shard_map/all_gather | solution.py:107
  7.9 107.1 %all-gather.14.cloned.1.call-start = ((), (), s32[]{:S(2)}) async-start(), calls=%async_computation.7 | async-start | bytes 2457600 | tf_op jit(solution)/shard_map/all_gather | solution.py:110
  8.7 199.4 %all-gather.16.cloned.1.call-start = ((), (), s32[]{:S(2)}) async-start(), calls=%async_computation.8 | async-start | bytes 6144000 | tf_op jit(solution)/shard_map/all_gather | solution.py:132
  9.4 291.2 %all-gather.18.cloned.1.call-start = ((), (), s32[]{:S(2)}) async-start(), calls=%async_computation.9 | async-start | bytes 6144000 | tf_op jit(solution)/shard_map/all_gather | solution.py:133
  10.0 383.1 %all-gather.20.cloned.1.call-start = ((), (), s32[]{:S(2)}) async-start(), calls=%async_computation.10 | async-start | bytes 6144000 | tf_op jit(solution)/shard_map/all_gather | solution.py:134
  10.6 524.3 %reduce-scatter.13.cloned.1.call-start = ((), (), s32[]{:S(2)}) async-start(), calls=%async_computation.16 | async-start | bytes 1843200 | tf_op jit(solution)/shard_map/reduce_scatter | solution.py:221
  79.0 133.6 %copy-start.13 = (bf16[5,64,3,128]{3,1,2,0:T(8,128)(2,1)}, bf16[5,64,3,128]{3,1,2,0:T(8,128)(2,1)S(1)}, u32[]{:S(2)}) copy-start(bf16[5,64,3,128]{3,1,2,0:T(8,128)(2,1)S(1)} %convolution_convert_fusion.1) | copy-start | bytes 737284
  118.0 90.1 %copy-start.43 = (f32[128]{0:T(128)}, f32[128]{0:T(128)S(1)}, u32[]{:S(2)}) copy-start(f32[128]{0:T(128)S(1)} %get-tuple-element.79) | copy-start | bytes 1540
  212.5 180.6 %copy-start.17 = (bf16[128,960]{0,1:T(8,128)(2,1)S(1)}, bf16[128,960]{0,1:T(8,128)(2,1)}, u32[]{:S(2)}) copy-start(bf16[128,960]{0,1:T(8,128)(2,1)} %param.23) | copy-start | bytes 737284
  414.5 121.7 %reduce-scatter.15.cloned.1.call-start = ((), (), s32[]{:S(2)}) async-start(), calls=%async_computation.17 | async-start | bytes 1843200 | tf_op jit(solution)/shard_map/reduce_scatter | solution.py:222
  417.3 149.4 %all-gather.22.cloned.1.call-start = ((), (), s32[]{:S(2)}) async-start(), calls=%async_computation.13 | async-start | bytes 3276800 | tf_op jit(solution)/shard_map/all_gather | solution.py:162
  418.0 203.7 %all-gather.24.cloned.1.call-start = ((), (), s32[]{:S(2)}) async-start(), calls=%async_computation.14 | async-start | bytes 3276800 | tf_op jit(solution)/shard_map/all_gather | solution.py:163
  418.8 276.6 %reduce-scatter.9.cloned.1.call-start = ((), (), s32[]{:S(2)}) async-start(), calls=%async_computation.11 | async-start | bytes 4915200 | tf_op jit(solution)/shard_map/reduce_scatter | solution.py:220
  424.4 346.4 %reduce-scatter.11.cloned.1.call-start = ((), (), s32[]{:S(2)}) async-start(), calls=%async_computation.12 | async-start | bytes 4915200 | tf_op jit(solution)/shard_map/reduce_scatter | solution.py:223
  427.9 66.3 %copy-start.10 = (bf16[960,320]{0,1:T(8,128)(2,1)S(1)}, bf16[960,320]{0,1:T(8,128)(2,1)}, u32[]{:S(2)}) copy-start(bf16[960,320]{0,1:T(8,128)(2,1)} %copy-done.9) | copy-start | bytes 1843204
  428.8 85.5 %copy-start.2 = (bf16[960,960]{1,0:T(8,128)(2,1)S(1)}, bf16[960,960]{1,0:T(8,128)(2,1)}, u32[]{:S(2)}) copy-start(bf16[960,960]{1,0:T(8,128)(2,1)} %all-gather.12.cloned.1.call-done) | copy-start | bytes 5529604
  428.8 85.5 %copy-start.25 = (f32[960]{0:T(1024)S(1)}, f32[960]{0:T(1024)}, u32[]{:S(2)}) copy-start(f32[960]{0:T(1024)} %copy-done.23) | copy-start | bytes 11524
  428.8 85.5 %copy-start.41 = (f32[128]{0:T(128)S(1)}, f32[128]{0:T(128)}, u32[]{:S(2)}) copy-start(f32[128]{0:T(128)} %copy-done.39) | copy-start | bytes 1540
  428.8 68.8 %all-to-all-start.1 = ((bf16[128,4,640]{2,0,1:T(8,128)(2,1)}), bf16[128,4,640]{2,0,1:T(8,128)(2,1)}, u32[]{:S(2)}, u32[]{:S(2)}) async-start(bf16[128,4,640]{2,0,1:T(8,128)(2,1)} %bitcast.127), calls=%async_computation.3 | async-start | bytes 1310720 | tf_op jit(solution)/shard_map/all_to_all | solution.py:160
  433.8 62.5 %copy-start.12 = (bf16[960,320]{0,1:T(8,128)(2,1)S(1)}, bf16[960,320]{0,1:T(8,128)(2,1)}, u32[]{:S(2)}) copy-start(bf16[960,320]{0,1:T(8,128)(2,1)} %copy-done.11) | copy-start | bytes 1843204
  497.6 40.4 %all-to-all-start = ((bf16[128,4,240]{0,2,1:T(8,128)(2,1)}), bf16[128,4,240]{0,2,1:T(8,128)(2,1)}, u32[]{:S(2)}, u32[]{:S(2)}) async-start(bf16[128,4,240]{0,2,1:T(8,128)(2,1)} %bitcast.39), calls=%async_computation.2 | async-start | bytes 491520 | tf_op jit(solution)/shard_map/all_to_all | solution.py:159
  514.4 493.5 %all-reduce.10.cloned.1.call-start = ((), (), s32[]{:S(2)}) async-start(), calls=%async_computation.18 | async-start | bytes 19668992
  626.0 147.3 %copy-start.1 = (f32[614400]{0:T(1024)S(1)}, f32[614400]{0:T(1024)}, u32[]{:S(2)}) copy-start(f32[614400]{0:T(1024)} %reshape.275) | copy-start | bytes 7372804
  864.2 212.6 %all-gather.26.cloned.1.call-start = ((), (), s32[]{:S(2)}) async-start(), calls=%async_computation.15 | async-start | bytes 11063808 | tf_op jit(solution)/shard_map/all_gather | solution.py:242
  (43 other events, 516.1 us)
Sparse Core Ops, SparseCore 0:
  9.6 59.6 all-gather.11
  70.8 44.0 all-gather.13
  116.5 91.4 all-gather.15
  209.5 91.0 all-gather.17
  302.0 91.0 all-gather.19
  414.6 39.8 reduce-scatter.12
  457.6 44.5 reduce-scatter.14
  504.3 62.3 all-gather.21
  568.2 53.4 all-gather.23
  623.9 71.4 reduce-scatter.8
  697.7 73.0 reduce-scatter.10
  864.3 143.4 all-reduce.9
  1016.2 60.5 all-gather.25
where the time goes:
time: 1120 us; the launch traced here: 1110 us
  waiting for transfers between devices  724 us (65%)
  local copies, waits for them, and re-layouts  151 us (13%)
  blocking collectives  131 us (12%)
  matrix products  63.1 us (6%)
  starting transfers between devices  22 us (2%)
  between operations  16.7 us (1%)
    unnamed x14, waiting for transfers between devices  146 us
    all_gather x1, waiting for transfers between devices, on_device(): lax.all_gather(gate_weight, 'shard', axis=0, tiled=True)  89.2 us
    all_gather x1, waiting for transfers between devices, on_device(): lax.all_gather(up_weight, 'shard', axis=0, tiled=True)  88.1 us
    all_gather x1, waiting for transfers between devices, on_device(): lax.all_gather(down_weight, 'shard', axis=0, tiled=True)  88.1 us
    concatenate x1, local copies, waits for them, and re-layouts, on_device(): flat_grads = jnp.concatenate([member.reshape(-1) for member in members])  81.9 us
    reduce_scatter x1, waiting for transfers between devices, on_device(): lax.psum_scatter(output_sum, 'shard', scatter_dimension=0, tiled=True)  72.8 us
    reduce_scatter x1, waiting for transfers between devices, on_device(): lax.psum_scatter(query_sum, 'shard', scatter_dimension=0, tiled=True)  69.3 us
    all_gather x1, blocking collectives, on_device(): cot_piece = lax.all_gather(out_grad, 'shard', axis=0, tiled=True)  60.4 us
  transfers between devices with their start and end apart: 15, of which 10 were waited for; matrix products, arithmetic and copies ran while one was open for 6% of the time, Pallas kernels for 0%

commit v1 on v0

--- a/solution.py
+++ b/solution.py
@@ -79,6 +79,87 @@
         "tkhd,skd->khts", query_rot, key_rot, preferred_element_type=jnp.float32
     )
     return jnp.where(allowed[None, None], raw_scores * score_scale, -1e30)
+
+
+def gather_weights(*shards):
+    return tuple(lax.all_gather(shard, "shard", axis=0, tiled=True) for shard in shards)
+
+
+def weight_grads(
+    normed_one, context, normed_two, out_grad, qkv_back, attn_low, gate_back, up_back, act
+):
+    n_replica = lax.axis_size("replica")
+    n_shard = lax.axis_size("shard")
+    count, width = normed_one.shape
+    ff = act.shape[1]
+    kv_width = KV_HEADS * HEAD
+
+    def over_copies(rows):
+        return lax.all_gather(rows, "replica", axis=0, tiled=True)
+
+    def parts(columns):
+        return columns.reshape(count, n_replica, -1)
+
+    act_parts = act.reshape(count, n_shard, n_replica, -1).swapaxes(1, 2)
+    columns = jnp.concatenate(
+        [
+            parts(gate_back),
+            parts(up_back),
+            act_parts.reshape(count, n_replica, -1),
+            parts(qkv_back),
+            parts(attn_low),
+        ],
+        axis=2,
+    )
+    columns = lax.all_to_all(columns, "replica", split_axis=1, concat_axis=0, tiled=True)
+    columns = columns.reshape(n_replica * count, -1)
+    ff_part = ff // n_replica
+    qkv_part = qkv_back.shape[1] // n_replica
+    out_part = width // n_replica
+    cuts = [0, 2 * ff_part, 3 * ff_part, 3 * ff_part + qkv_part, columns.shape[1]]
+    gate_up, act_cols, qkv_cols, out_cols = (
+        columns[:, low:high] for low, high in zip(cuts[:-1], cuts[1:])
+    )
+    row_part = jnp.concatenate(
+        [
+            matmul_left_t(over_copies(normed_two), gate_up),
+            matmul_left_t(over_copies(normed_one), qkv_cols),
+            matmul_left_t(over_copies(context), out_cols),
+        ],
+        axis=1,
+    ).astype(jnp.bfloat16)
+    down_part = matmul_left_t(act_cols, over_copies(out_grad)).astype(jnp.bfloat16)
+    own_rows = width // n_shard
+    down_rows = ff_part // n_shard
+    row_terms = lax.all_to_all(
+        row_part.reshape(n_shard, own_rows, -1), "shard", split_axis=0, concat_axis=0, tiled=True
+    )
+    down_terms = lax.all_to_all(
+        down_part.reshape(n_shard, down_rows, width),
+        "shard",
+        split_axis=0,
+        concat_axis=0,
+        tiled=True,
+    )
+    row_own = jnp.sum(row_terms.astype(jnp.float32), axis=0).astype(jnp.bfloat16)
+    down_own = jnp.sum(down_terms.astype(jnp.float32), axis=0).astype(jnp.bfloat16)
+    row_all = lax.all_gather(row_own, "replica", axis=0)
+    down_all = lax.all_gather(down_own, "replica", axis=0, tiled=True)
+
+    def whole(low, high):
+        piece = row_all[:, :, low:high].swapaxes(0, 1).astype(jnp.float32)
+        return piece.reshape(own_rows, -1)
+
+    qkv_grad = whole(2 * ff_part, 2 * ff_part + qkv_part)
+    return (
+        qkv_grad[:, :width],
+        qkv_grad[:, width : width + kv_width],
+        qkv_grad[:, width + kv_width :],
+        whole(2 * ff_part + qkv_part, 2 * ff_part + qkv_part + out_part),
+        whole(0, ff_part),
+        whole(ff_part, 2 * ff_part),
+        down_all.astype(jnp.float32),
+    )
 
 
 def on_device(
@@ -102,37 +183,35 @@
     cosine, sine = tables(positions, HEAD)
     slots = jnp.arange(count, dtype=jnp.int32)
     allowed = (doc_index[:, None] == doc_index[None, :]) & (slots[:, None] >= slots[None, :])
-    gain_one, wide_query, wide_key, wide_value, wide_output = (
-        lax.all_gather(norm_one, "shard", axis=0, tiled=True),
-        lax.all_gather(query_weight, "shard", axis=0, tiled=True),
-        lax.all_gather(key_weight, "shard", axis=0, tiled=True),
-        lax.all_gather(value_weight, "shard", axis=0, tiled=True),
-        lax.all_gather(output_weight, "shard", axis=0, tiled=True),
+    gain_one, gain_two, wide_qkv, wide_output, wide_gate, wide_up, wide_down = gather_weights(
+        norm_one,
+        norm_two,
+        jnp.concatenate([query_weight, key_weight, value_weight], axis=1),
+        output_weight,
+        gate_weight,
+        up_weight,
+        down_weight,
     )
     hidden_in = tokens.astype(jnp.float32)
     scale_one = lax.rsqrt(jnp.mean(hidden_in * hidden_in, axis=-1, keepdims=True) + EPSILON)
     normed_one = (hidden_in * scale_one * gain_one.astype(jnp.float32)).astype(jnp.bfloat16)
-    queries_pre = matmul(normed_one, wide_query).reshape(count, HEADS, HEAD)
+    qkv_pre = matmul(normed_one, wide_qkv)
+    kv_width = KV_HEADS * HEAD
+    queries_pre = qkv_pre[:, :width].reshape(count, HEADS, HEAD)
     query_rot = (
         rotate(queries_pre, cosine, sine)
         .astype(jnp.bfloat16)
         .reshape(count, KV_HEADS, group_heads, HEAD)
     )
-    keys_pre = matmul(normed_one, wide_key).reshape(count, KV_HEADS, HEAD)
+    keys_pre = qkv_pre[:, width : width + kv_width].reshape(count, KV_HEADS, HEAD)
     key_rot = rotate(keys_pre, cosine, sine).astype(jnp.bfloat16)
-    value_rot = matmul(normed_one, wide_value).astype(jnp.bfloat16).reshape(count, KV_HEADS, HEAD)
+    value_rot = qkv_pre[:, width + kv_width :].astype(jnp.bfloat16).reshape(count, KV_HEADS, HEAD)
     scores = masked_scores(query_rot, key_rot, allowed, score_scale)
     log_total = jax.nn.logsumexp(scores, axis=-1, keepdims=True)
     probs_low = jnp.exp(scores - log_total).astype(jnp.bfloat16)
     context = jnp.einsum("khts,skd->tkhd", probs_low, value_rot, preferred_element_type=jnp.float32)
     context = context.reshape(count, width).astype(jnp.bfloat16)
     after_attn = hidden_in + matmul(context, wide_output)
-    gain_two, wide_gate, wide_up, wide_down = (
-        lax.all_gather(norm_two, "shard", axis=0, tiled=True),
-        lax.all_gather(gate_weight, "shard", axis=0, tiled=True),
-        lax.all_gather(up_weight, "shard", axis=0, tiled=True),
-        lax.all_gather(down_weight, "shard", axis=0, tiled=True),
-    )
     scale_two = lax.rsqrt(jnp.mean(after_attn * after_attn, axis=-1, keepdims=True) + EPSILON)
     normed_two = (after_attn * scale_two * gain_two.astype(jnp.float32)).astype(jnp.bfloat16)
     gate_pre = matmul(normed_two, wide_gate)
@@ -155,20 +234,7 @@
         + scale_two * weighted_two
         - after_attn * scale_two**3 * jnp.mean(after_attn * weighted_two, axis=-1, keepdims=True)
     )
-    normed_cols, act_cols = (
-        lax.all_to_all(normed_two, "shard", split_axis=1, concat_axis=0, tiled=True),
-        lax.all_to_all(act, "shard", split_axis=1, concat_axis=0, tiled=True),
-    )
-    gate_piece = lax.all_gather(gate_back, "shard", axis=0, tiled=True)
-    up_piece = lax.all_gather(up_back, "shard", axis=0, tiled=True)
-    cot_piece = lax.all_gather(out_grad, "shard", axis=0, tiled=True)
-    gate_own = matmul_left_t(normed_cols, gate_piece)
-    up_own = matmul_left_t(normed_cols, up_piece)
-    down_own = matmul_left_t(act_cols, cot_piece)
-    gain_two_own = lax.psum_scatter(gain_two_sum, "shard", scatter_dimension=0, tiled=True)
-    feed_shards = (gain_two_own, gate_own, up_own, down_own)
     attn_low = attn_out_grad.astype(jnp.bfloat16)
-    output_sum = matmul_left_t(context, attn_low)
     context_grad = (
         matmul_right_t(attn_low, wide_output)
         .astype(jnp.bfloat16)
@@ -200,14 +266,8 @@
     key_back = (
         unrotate(key_rot_grad, cosine, sine).reshape(count, KV_HEADS * HEAD).astype(jnp.bfloat16)
     )
-    query_sum = matmul_left_t(normed_one, query_back)
-    key_sum = matmul_left_t(normed_one, key_back)
-    value_sum = matmul_left_t(normed_one, value_back)
-    normed_one_grad = (
-        matmul_right_t(query_back, wide_query)
-        + matmul_right_t(key_back, wide_key)
-        + matmul_right_t(value_back, wide_value)
-    )
+    qkv_back = jnp.concatenate([query_back, key_back, value_back], axis=1)
+    normed_one_grad = matmul_right_t(qkv_back, wide_qkv)
     gain_one_sum = jnp.sum(normed_one_grad * hidden_in * scale_one, axis=0)
     weighted_one = normed_one_grad * gain_one.astype(jnp.float32)
     input_grad = (
@@ -215,48 +275,26 @@
         + scale_one * weighted_one
         - hidden_in * scale_one**3 * jnp.mean(hidden_in * weighted_one, axis=-1, keepdims=True)
     )
-    attn_shards = (
-        lax.psum_scatter(gain_one_sum, "shard", scatter_dimension=0, tiled=True),
-        lax.psum_scatter(query_sum, "shard", scatter_dimension=0, tiled=True),
-        lax.psum_scatter(key_sum, "shard", scatter_dimension=0, tiled=True),
-        lax.psum_scatter(value_sum, "shard", scatter_dimension=0, tiled=True),
-        lax.psum_scatter(output_sum, "shard", scatter_dimension=0, tiled=True),
-    )
-    members = (
-        attn_shards[0],
-        attn_shards[1],
-        attn_shards[2],
-        attn_shards[3],
-        attn_shards[4],
-        feed_shards[0],
-        feed_shards[1],
-        feed_shards[2],
-        feed_shards[3],
-    )
-    flat_grads = jnp.concatenate([member.reshape(-1) for member in members])
-    used_len = flat_grads.shape[0]
-    tile_span = lax.axis_size("replica") * 128
-    padded_len = -(-used_len // tile_span) * tile_span
-    flat_grads = jnp.pad(flat_grads, (0, padded_len - used_len))
-    own_part = lax.psum_scatter(flat_grads, "replica", scatter_dimension=0, tiled=True)
-    whole_sum = lax.all_gather(own_part, "replica", axis=0, tiled=True)
-    unpacked = []
-    offset = 0
-    for member in members:
-        unpacked.append(whole_sum[offset : offset + member.size].reshape(member.shape))
-        offset = offset + member.size
+    gain_sums = lax.psum(jnp.stack([gain_one_sum, gain_two_sum]), ("replica", "shard"))
+    own_rows = width // lax.axis_size("shard")
+    gain_own = lax.dynamic_slice_in_dim(
+        gain_sums, lax.axis_index("shard") * own_rows, own_rows, axis=1
+    )
+    grads = weight_grads(
+        normed_one, context, normed_two, out_grad, qkv_back, attn_low, gate_back, up_back, act
+    )
     return (
         mixed,
         input_grad,
-        unpacked[0],
-        unpacked[1],
-        unpacked[2],
-        unpacked[3],
-        unpacked[4],
-        unpacked[5],
-        unpacked[6],
-        unpacked[7],
-        unpacked[8],
+        gain_own[0],
+        grads[0],
+        grads[1],
+        grads[2],
+        grads[3],
+        gain_own[1],
+        grads[4],
+        grads[5],
+        grads[6],
     )
 
 

time: 1120 us -> 672 us (0.60)
  waiting for transfers between devices: 724 us -> 438 us
  local copies, waits for them, and re-layouts: 151 us -> 43.7 us
  blocking collectives: 131 us -> 94.5 us
  starting transfers between devices: 22 us -> 9.61 us
    unnamed x14 -> x11, waiting for transfers between devices: 146 us -> 3.05 us
    reduce_scatter x4 -> x0, waiting for transfers between devices: 142 us -> none  [the longest x1 72.8 us: on_device(): lax.psum_scatter(output_sum, 'shard', scatter_dimension=0, tiled=True)]
    all_gather x3 -> x0, blocking collectives: 106 us -> none  [the longest x1 60.4 us: on_device(): cot_piece = lax.all_gather(out_grad, 'shard', axis=0, tiled=True)]
    concatenate x1 -> x3, local copies, waits for them, and re-layouts: 81.9 us -> 3.73 us  [the longest x1 1.96 us: on_device(): jnp.concatenate([query_weight, key_weight, value_weight], axis=1)]
    all_gather x8 -> x11, waiting for transfers between devices: 436 us -> 391 us  [the longest x5 350 us: gather_weights(): lax.all_gather(shard, 'shard', axis=0, tiled=True)]
    all_to_all x0 -> x1, blocking collectives: none -> 43.6 us  [weight_grads(): lax.all_to_all(columns, 'replica', split_axis=1, concat_axis=0, tiled=True)]
    all_to_all x2, waiting for transfers between devices: 0.01 us -> 43.6 us  [the longest x1 43.6 us: weight_grads(): lax.all_to_all(row_part.reshape(n_shard, own_rows, -1), 'shard', split_ax...]
    psum x0 -> x1, blocking collectives: none -> 37.1 us  [on_device(): lax.psum(jnp.stack([gain_one_sum, gain_two_sum]), ('replica', 'shard'))]
  transfers between devices with their start and end apart: 15 -> 13, of which waited for: 10 -> 8; matrix products, arithmetic and copies ran while one was open for 6% -> 12% of each run, Pallas kernels for 0% -> 0%
where the time goes in v1:
time: 672 us; the launch traced here: 670 us
  waiting for transfers between devices  438 us (65%)
  blocking collectives  94.5 us (14%)
  matrix products  56.2 us (8%)
  local copies, waits for them, and re-layouts  43.7 us (7%)
  between operations  15.4 us (2%)
  other arithmetic  12.9 us (2%)
  starting transfers between devices  9.61 us (1%)
    all_gather x5, waiting for transfers between devices, gather_weights(): lax.all_gather(shard, 'shard', axis=0, tiled=True)  350 us
    all_to_all x1, blocking collectives, weight_grads(): lax.all_to_all(columns, 'replica', split_axis=1, concat_axis=0, tiled=True)  43.6 us
    all_to_all x1, waiting for transfers between devices, weight_grads(): lax.all_to_all(row_part.reshape(n_shard, own_rows, -1), 'shard', split_ax...  43.6 us
    all_gather x4, waiting for transfers between devices, over_copies(): return lax.all_gather(rows, 'replica', axis=0, tiled=True)  41.9 us
    psum x1, blocking collectives, on_device(): lax.psum(jnp.stack([gain_one_sum, gain_two_sum]), ('replica', 'shard'))  37.1 us
    unnamed x116, local copies, waits for them, and re-layouts  24 us
    dot_general x5, matrix products, matmul(): return jnp.dot(left, right, preferred_element_type=jnp.float32)  19.4 us
    dot_general x5, matrix products, matmul_right_t(): jnp.einsum('te,de->td', left, right, preferred_element_type=jnp.float32)  14.7 us
  transfers between devices with their start and end apart: 13, of which 8 were waited for; matrix products, arithmetic and copies ran while one was open for 12% of the time, Pallas kernels for 0%

profile of v1, /device:TPU:0, one launch (start us, length us, event | category | flops | bytes accessed | tf_op | source)
XLA Modules:
  0.0 670.3 jit_solution(14027253663463471062)
XLA Ops:
  16.4 13.7 %all-reduce.2 = (bf16[960]{0:T(1024)(128)(2,1)S(1)}, bf16[960]{0:T(1024)(128)(2,1)S(1)}) all-reduce(bf16[960]{0:T(1024)(128)(2,1)S(1)} %dynamic-update-slice, bf16[960]{0:T(1024)(128)(2,1)S(1)} %dynamic-update-slice.1), channel_id=1, replica_groups=mesh['replica'=8,'shard'=4] {'shard'}, use_global_device_ids=true, to_apply=%add | all-reduce | flops 1920 | bytes 7680
  32.4 46.2 %all-gather.13.cloned.1.call-done = bf16[960,1600]{1,0:T(8,128)(2,1)} async-done(((bf16[240,1600]{1,0:T(8,128)(2,1)}), bf16[960,1600]{1,0:T(8,128)(2,1)}) %all-gather.13.cloned.1.call-update) | async-done | bytes 3072016 | tf_op jit(solution)/shard_map/all_gather | solution.py:85
  78.6 3.5 fusion.52
  84.3 38.1 %all-gather.15.cloned.1.call-done = bf16[960,960]{1,0:T(8,128)(2,1)} async-done(((bf16[240,960]{1,0:T(8,128)(2,1)}), bf16[960,960]{1,0:T(8,128)(2,1)}) %all-gather.15.cloned.1.call-update) | async-done | bytes 1843216 | tf_op jit(solution)/shard_map/all_gather | solution.py:85
  126.5 89.0 %all-gather.17.cloned.1.call-done = bf16[960,2560]{1,0:T(8,128)(2,1)} async-done(((bf16[240,2560]{1,0:T(8,128)(2,1)}), bf16[960,2560]{1,0:T(8,128)(2,1)}) %all-gather.17.cloned.1.call-update) | async-done | bytes 4915216 | tf_op jit(solution)/shard_map/all_gather | solution.py:85
  215.5 4.5 fusion.53
  220.0 88.1 %all-gather.19.cloned.1.call-done = bf16[960,2560]{1,0:T(8,128)(2,1)} async-done(((bf16[240,2560]{1,0:T(8,128)(2,1)}), bf16[960,2560]{1,0:T(8,128)(2,1)}) %all-gather.19.cloned.1.call-update) | async-done | bytes 4915216 | tf_op jit(solution)/shard_map/all_gather | solution.py:85
  308.1 4.3 fusion.54
  312.4 88.2 %all-gather.21.cloned.1.call-done = bf16[2560,960]{0,1:T(8,128)(2,1)} async-done(((bf16[640,960]{0,1:T(8,128)(2,1)}), bf16[2560,960]{0,1:T(8,128)(2,1)}) %all-gather.21.cloned.1.call-update) | async-done | bytes 4915216 | tf_op jit(solution)/shard_map/all_gather | solution.py:85
  400.6 4.6 multiply_convert_fusion
  405.2 4.2 fusion.55
  418.2 3.1 convolution_bitcast_fusion.2
  431.2 43.6 %all_to_all.25 = bf16[128,8,1280]{0,2,1:T(8,128)(2,1)S(1)} all-to-all(bf16[128,8,1280]{0,2,1:T(8,128)(2,1)} %constant_dynamic-update-slice_fusion), channel_id=1, replica_groups=mesh['replica'=8,'shard'=4] {'replica'}, dimensions={1} | all-to-all | bytes 5242880 | tf_op jit(solution)/shard_map/all_to_all | solution.py:114
  477.4 4.0 convolution_convert_fusion.1
  481.4 4.4 all-to-all-start.2
  489.3 14.0 %all-gather.27.cloned.1.call-done = bf16[1024,960]{0,1:T(8,128)(2,1)} async-done(((bf16[128,960]{0,1:T(8,128)(2,1)}), bf16[1024,960]{0,1:T(8,128)(2,1)}) %all-gather.27.cloned.1.call-update) | async-done | bytes 1966096 | tf_op jit(solution)/shard_map/all_gather | solution.py:98
  505.7 27.8 %all-gather.23.cloned.1.call-done = bf16[1024,960]{0,1:T(8,128)(2,1)} async-done(((bf16[128,960]{0,1:T(8,128)(2,1)}), bf16[1024,960]{0,1:T(8,128)(2,1)}) %all-gather.23.cloned.1.call-update) | async-done | bytes 1966096 | tf_op jit(solution)/shard_map/all_gather | solution.py:98
  533.5 3.3 convolution_convert_fusion
  538.4 4.6 all-to-all-start.1
  545.3 43.6 %all-to-all-done.1 = bf16[4,240,960]{2,1,0:T(8,128)(2,1)S(1)} async-done(((bf16[4,240,960]{2,1,0:T(8,128)(2,1)}), bf16[4,240,960]{2,1,0:T(8,128)(2,1)S(1)}, u32[]{:S(2)}, u32[]{:S(2)}) %all-to-all-start.1) | async-done | bytes 1843232 | tf_op jit(solution)/shard_map/all_to_all | solution.py:134
  590.3 3.1 fusion.27
  593.4 37.1 %psum.7 = f32[2,960]{1,0:T(2,128)S(1)} all-reduce(f32[2,960]{1,0:T(2,128)S(1)} %pad_maximum_fusion.7), channel_id=1, replica_groups=mesh['replica'=8,'shard'=4] {'replica','shard'}, use_global_device_ids=true, to_apply=%region_12.13 | all-reduce | flops 1920 | bytes 15360 | tf_op jit(solution)/shard_map/psum | solution.py:278
  632.3 4.5 fusion.9
  639.6 3.8 fusion.48
  (210 shorter events, 73.6 us)
Async XLA Ops:
  7.2 71.4 %all-gather.13.cloned.1.call-start = ((), (), s32[]{:S(2)}) async-start(), calls=%async_computation.3 | async-start | bytes 3993600 | tf_op jit(solution)/shard_map/all_gather | solution.py:85
  11.4 111.1 %all-gather.15.cloned.1.call-start = ((), (), s32[]{:S(2)}) async-start(), calls=%async_computation.4 | async-start | bytes 2457600 | tf_op jit(solution)/shard_map/all_gather | solution.py:85
  12.2 203.4 %all-gather.17.cloned.1.call-start = ((), (), s32[]{:S(2)}) async-start(), calls=%async_computation.5 | async-start | bytes 6144000 | tf_op jit(solution)/shard_map/all_gather | solution.py:85
  12.9 295.2 %all-gather.19.cloned.1.call-start = ((), (), s32[]{:S(2)}) async-start(), calls=%async_computation.6 | async-start | bytes 6144000 | tf_op jit(solution)/shard_map/all_gather | solution.py:85
  13.5 387.1 %all-gather.21.cloned.1.call-start = ((), (), s32[]{:S(2)}) async-start(), calls=%async_computation.7 | async-start | bytes 6144000 | tf_op jit(solution)/shard_map/all_gather | solution.py:85
  14.1 463.4 %all-gather.29.cloned.1.call-start = ((), (), s32[]{:S(2)}) async-start(), calls=%async_computation.11 | async-start | bytes 2211840 | tf_op jit(solution)/shard_map/all_gather | solution.py:98
  14.6 471.2 %all-gather.25.cloned.1.call-start = ((), (), s32[]{:S(2)}) async-start(), calls=%async_computation.9 | async-start | bytes 2211840 | tf_op jit(solution)/shard_map/all_gather | solution.py:98
  31.8 471.6 %all-gather.27.cloned.1.call-start = ((), (), s32[]{:S(2)}) async-start(), calls=%async_computation.10 | async-start | bytes 2211840 | tf_op jit(solution)/shard_map/all_gather | solution.py:98
  83.0 42.0 %copy-start.28 = (f32[5,3,128]{2,1,0:T(4,128)}, f32[5,3,128]{2,1,0:T(4,128)S(1)}, u32[]{:S(2)}) copy-start(f32[5,3,128]{2,1,0:T(4,128)S(1)} %log_add_fusion) | copy-start | bytes 23044
  84.1 449.4 %all-gather.23.cloned.1.call-start = ((), (), s32[]{:S(2)}) async-start(), calls=%async_computation.8 | async-start | bytes 2211840 | tf_op jit(solution)/shard_map/all_gather | solution.py:98
  84.3 42.2 %copy-start.25 = (f32[960]{0:T(1024)}, f32[960]{0:T(1024)S(1)}, u32[]{:S(2)}) copy-start(f32[960]{0:T(1024)S(1)} %convert_element_type.122) | copy-start | bytes 11524
  125.6 94.4 %copy-start.34 = (f32[128]{0:T(128)}, f32[128]{0:T(128)S(1)}, u32[]{:S(2)}) copy-start(f32[128]{0:T(128)S(1)} %get-tuple-element.94) | copy-start | bytes 1540
  126.5 181.6 %copy-start.4 = (bf16[128,960]{0,1:T(8,128)(2,1)S(1)}, bf16[128,960]{0,1:T(8,128)(2,1)}, u32[]{:S(2)}) copy-start(bf16[128,960]{0,1:T(8,128)(2,1)} %multiply_convert_fusion.3) | copy-start | bytes 737284
  481.4 57.0 %all-to-all-start.2 = ((bf16[4,80,960]{2,1,0:T(8,128)(2,1)}), bf16[4,80,960]{2,1,0:T(8,128)(2,1)}, u32[]{:S(2)}, u32[]{:S(2)}) async-start(bf16[4,80,960]{2,1,0:T(8,128)(2,1)} %bitcast.144), calls=%async_computation.2 | async-start | bytes 1310720 | tf_op jit(solution)/shard_map/all_to_all | solution.py:137
  538.4 50.4 %all-to-all-start.1 = ((bf16[4,240,960]{2,1,0:T(8,128)(2,1)}), bf16[4,240,960]{2,1,0:T(8,128)(2,1)S(1)}, u32[]{:S(2)}, u32[]{:S(2)}) async-start(bf16[4,240,960]{2,1,0:T(8,128)(2,1)} %pad_maximum_fusion), calls=%async_computation.1 | async-start | bytes 3932160 | tf_op jit(solution)/shard_map/all_to_all | solution.py:134
  543.0 47.1 %copy-start.6 = (bf16[128,960]{0,1:T(8,128)(2,1)S(1)}, bf16[128,960]{0,1:T(8,128)(2,1)}, u32[]{:S(2)}) copy-start(bf16[128,960]{0,1:T(8,128)(2,1)} %param.12) | copy-start | bytes 737284
  543.0 47.1 %copy-start.18 = (bf16[128,15,64]{0,2,1:T(8,128)(2,1)S(1)}, bf16[128,15,64]{0,2,1:T(8,128)(2,1)}, u32[]{:S(2)}) copy-start(bf16[128,15,64]{0,2,1:T(8,128)(2,1)} %copy-done.17) | copy-start | bytes 737284
  543.0 47.1 %copy-start.20 = (bf16[5,64,128]{2,1,0:T(8,128)(2,1)S(1)}, bf16[5,64,128]{2,1,0:T(8,128)(2,1)}, u32[]{:S(2)}) copy-start(bf16[5,64,128]{2,1,0:T(8,128)(2,1)} %copy-done.19) | copy-start | bytes 245764
  543.0 47.1 %copy-start.22 = (bf16[128,5,64]{0,2,1:T(8,128)(2,1)S(1)}, bf16[128,5,64]{0,2,1:T(8,128)(2,1)}, u32[]{:S(2)}) copy-start(bf16[128,5,64]{0,2,1:T(8,128)(2,1)} %copy-done.21) | copy-start | bytes 245764
  543.1 47.1 %copy-start.32 = (f32[960]{0:T(1024)S(1)}, f32[960]{0:T(1024)}, u32[]{:S(2)}) copy-start(f32[960]{0:T(1024)} %copy-done.31) | copy-start | bytes 11524
  543.1 47.1 %copy-start.38 = (f32[128]{0:T(128)S(1)}, f32[128]{0:T(128)}, u32[]{:S(2)}) copy-start(f32[128]{0:T(128)} %copy-done.37) | copy-start | bytes 1540
  543.1 93.7 %all-gather.31.cloned.1.call-start = ((), (), s32[]{:S(2)}) async-start(), calls=%async_computation.12 | async-start | bytes 1474560 | tf_op jit(solution)/shard_map/all_gather | solution.py:147
  545.2 94.4 %all-gather.33.cloned.1.call-start = ((), (), s32[]{:S(2)}) async-start(), calls=%async_computation.13 | async-start | bytes 4423680 | tf_op jit(solution)/shard_map/all_gather | solution.py:146
  590.2 40.9 %copy-start.3 = (f32[128,960]{0,1:T(8,128)S(1)}, f32[128,960]{0,1:T(8,128)}, u32[]{:S(2)}) copy-start(f32[128,960]{0,1:T(8,128)} %copy-done.2) | copy-start | bytes 1474564
  (37 other events, 418.0 us)
Sparse Core Ops, SparseCore 0:
  11.5 67.0 all-gather.12
  80.2 42.1 all-gather.14
  124.0 91.4 all-gather.16
  216.9 91.0 all-gather.18
  309.5 91.0 all-gather.20
  402.3 26.0 all-gather.28
  430.8 43.2 all-gather.24
  476.6 26.6 all-gather.26
  505.8 27.6 all-gather.22
  546.1 25.0 all-gather.30
  590.3 34.0 all-gather.32
